TPU v7x, 128 devices: a whole 4x4x4 slice. The times are simulated.
128 devices in a mesh: grp: 4 (over y), mem: 32 (over x, z, core).
Axes of the slice: x: 4, y: 4, z: 4, core: 2. Of those that a mesh axis runs over, the one named last changes fastest.
Arguments:
- weights: bfloat16 [64, 1536, 4096], P('mem', None, 'grp'), may hold values from -0.09375 to 0.09375
- stored_order: int32 [64], replicated, may hold values from 0 to 63, each once
- assignment: int32 [64, 1], replicated, may hold values from 0 to 3; in each aligned block of 64 rows (0 to 63, 64 to 127, ...) at most 24 rows name the same one
- init_basis: bfloat16 [4, 4096, 512], P('grp'), may hold values from -6 to 6
Outputs:
- basis: bfloat16 [4, 4096, 512], P('grp', 'mem')
- coefficients: bfloat16 [4, 24, 1536, 512], P('grp', None, 'mem')
Inputs may be any that keep to these rules, and one draw needn't show every extreme that they name: `stored_order`: each expert id appears exactly once. `assignment`: every group has at least one expert and at most 24; some group has exactly 24.
All inputs are finite; a program needn't handle non-finite values.
Results may differ from a plain program's by a relative error of at most 0.024.
Values may be sent and summed in bfloat16 or wider, within the bound.
A program may use at most 192 MiB of HBM per device.

v0:
```python
import jax
import jax.numpy as jnp
from jax import lax
from jax.sharding import PartitionSpec as P

D = 4096
ITERS = 2
NS_STEPS = 6


def slot_picker(stored_order, assignment, groups, capacity, experts):
    assign = assignment[:, 0]
    member = (assign[None, :] == jnp.arange(groups, dtype=jnp.int32)[:, None]).astype(jnp.int32)
    ranking = jnp.cumsum(member, axis=1) - member
    slot_hit = (member[:, None, :] == 1) & (
        ranking[:, None, :] == jnp.arange(capacity, dtype=jnp.int32)[None, :, None]
    )
    holder = (stored_order[None, :] == jnp.arange(experts, dtype=jnp.int32)[:, None]).astype(
        jnp.float32
    )
    flat_hit = slot_hit.reshape(groups * capacity, experts).astype(jnp.float32)
    return jnp.dot(flat_hit, holder).astype(jnp.bfloat16)


def inverse_root(gram):
    rank_size = gram.shape[0]
    identity = jnp.eye(rank_size, dtype=jnp.float32)
    frob = jnp.sqrt(jnp.sum(gram * gram)) + 1e-06
    scaled = gram / frob
    root = identity
    for inner in range(NS_STEPS):
        factor = 1.5 * identity - 0.5 * jnp.dot(root, scaled, precision=lax.Precision.HIGHEST)
        scaled = jnp.dot(scaled, factor, precision=lax.Precision.HIGHEST)
        root = jnp.dot(factor, root, precision=lax.Precision.HIGHEST)
    return (root, frob)


def body(weights, stored_order, assignment, init_basis):
    groups = lax.axis_size("grp")
    members = lax.axis_size("mem")
    experts = weights.shape[0] * members
    capacity = experts // groups + experts // (2 * groups)
    moved = lax.all_to_all(weights, "mem", split_axis=1, concat_axis=0, tiled=True)
    columns = moved.shape[1]
    part_rows = moved.shape[2]
    picker = slot_picker(stored_order, assignment, groups, capacity, experts)
    selected = jnp.dot(
        picker, moved.reshape(experts, columns * part_rows), preferred_element_type=jnp.float32
    )
    outgoing = selected.astype(jnp.bfloat16).reshape(groups, capacity, columns, part_rows)
    arrived = lax.all_to_all(outgoing, "grp", split_axis=0, concat_axis=3, tiled=True)
    regrouped = arrived[0]
    start_full = init_basis[0]
    row_count = start_full.shape[0] // members
    full_basis = start_full
    for sweep in range(ITERS):
        projected = jnp.einsum(
            "kcd,dr->kcr", regrouped, full_basis, preferred_element_type=jnp.float32
        ).astype(jnp.bfloat16)
        partial_value = jnp.einsum(
            "kcd,kcr->dr", regrouped, projected, preferred_element_type=jnp.float32
        )
        image = lax.psum(partial_value.astype(jnp.bfloat16), "mem").astype(jnp.float32)
        gram = jnp.dot(image.T, image, precision=lax.Precision.HIGHEST)
        root, frob = inverse_root(gram)
        full_basis = (
            jnp.dot(image, root, precision=lax.Precision.HIGHEST) * jnp.sqrt(D / frob)
        ).astype(jnp.bfloat16)
    coefficients = jnp.einsum(
        "kcd,dr->kcr", regrouped, full_basis, preferred_element_type=jnp.float32
    ).astype(jnp.bfloat16)
    basis_out = lax.dynamic_slice_in_dim(
        full_basis, lax.axis_index("mem") * row_count, row_count, 0
    )
    return (basis_out[None], coefficients[None])


def solution(mesh):
    return jax.shard_map(
        body,
        mesh=mesh,
        in_specs=(P("mem", None, "grp"), P(), P(), P("grp", None, None)),
        out_specs=(P("grp", "mem", None), P("grp", None, "mem", None)),
        check_vma=False,
    )
```

profile of v0, /device:TPU:1, one launch (start us, length us, event | category | flops | bytes accessed | tf_op | source)
XLA Modules:
  0.0 689.3 jit_solution(13239976061336349387)
XLA Ops:
  7.2 12.6 %copy.9 = bf16[2,1536,1024]{2,0,1:T(2,128)(2,1)} copy(bf16[2,1536,1024]{2,1,0:T(8,128)(2,1)} %param.4) | data formatting | bytes 12582912 | tf_op args[0]
  19.8 9.6 %all-to-all-start = ((bf16[2,1536,1024]{2,0,1:T(2,128)(2,1)}), bf16[2,1536,1024]{2,0,1:T(2,128)(2,1)}, u32[]{:S(2)}, u32[]{:S(2)}) async-start(bf16[2,1536,1024]{2,0,1:T(2,128)(2,1)} %copy.9), calls=%async_computation | async-start | bytes 12582912 | tf_op jit(solution)/shard_map/all_to_all | solution.py:43
  29.9 77.5 %all-to-all-done = bf16[2,1536,1024]{2,0,1:T(2,128)(2,1)} async-done(((bf16[2,1536,1024]{2,0,1:T(2,128)(2,1)}), bf16[2,1536,1024]{2,0,1:T(2,128)(2,1)}, u32[]{:S(2)}, u32[]{:S(2)}) %all-to-all-start) | async-done | bytes 6291488 | tf_op jit(solution)/shard_map/all_to_all | solution.py:43
  107.4 4.9 copy.10
  112.4 6.5 copy.12
  118.8 9.3 %convolution_convert_fusion = bf16[96,49152]{1,0:T(8,128)(2,1)} fusion(bf16[64,49152]{1,0:T(8,128)(2,1)} %bitcast.122, pred[96,64]{1,0:T(32,128)(4,1)S(1)} %fusion.20, s32[64]{0:T(128)S(1)} %copy-done.1), kind=kOutput, calls=%fused_computation | convolution fusion | flops 609495040 | bytes 15735040 | tf_op jit(solution)/shard_map/dot_general | solution.py:47
  128.1 13.8 %copy.13 = bf16[12,8,48,1024]{3,2,1,0:T(8,128)(2,1)} copy(bf16[12,8,48,1024]{3,1,2,0:T(8,128)(2,1)} %bitcast.119) | data formatting | bytes 18874368
  141.9 106.8 %all_to_all.30 = bf16[4,24,48,1024]{3,2,1,0:T(8,128)(2,1)S(1)} all-to-all(bf16[4,24,48,1024]{3,2,1,0:T(8,128)(2,1)} %bitcast.120), channel_id=1, replica_groups=mesh['grp'=4,'mem'=32] {'grp'}, dimensions={0} | all-to-all | bytes 18874368 | tf_op jit(solution)/shard_map/all_to_all | solution.py:51
  248.7 21.9 %copy.11 = bf16[1,24,48,4,1024]{4,3,2,1,0:T(4,128)(2,1)} copy(bf16[1,24,48,4,1024]{4,2,1,3,0:T(8,128)(2,1)S(1)} %bitcast.121) | data formatting | bytes 18874368 | tf_op jit(solution)/shard_map/all_to_all | solution.py:51
  270.6 16.1 %squeeze.6 = bf16[24,48,4096]{2,1,0:T(8,128)(2,1)} reshape(bf16[1,24,48,4,1024]{4,3,2,1,0:T(4,128)(2,1)} %copy.11) | data formatting | bytes 18874368 | tf_op jit(solution)/shard_map/squeeze | solution.py:52
  286.7 29.2 %bitcast_convert_fusion.1 = bf16[4096,512]{1,0:T(8,128)(2,1)} fusion(bf16[24,48,4096]{2,1,0:T(8,128)(2,1)} %squeeze.6, bf16[1,4096,512]{2,1,0:T(8,128)(2,1)} %param.7), kind=kOutput, calls=%fused_computation.2 | convolution fusion | flops 9666363392 | bytes 17825792 | tf_op jit(solution)/shard_map/kcd,kcr->dr/dot_general | solution.py:60
  316.1 120.5 %all-reduce.3.cloned.1.call-done = bf16[4096,512]{1,0:T(8,128)(2,1)} async-done(((bf16[4096,512]{1,0:T(8,128)(2,1)}), bf16[4096,512]{1,0:T(8,128)(2,1)}) %all-reduce.3.cloned.1.call-update) | async-done | bytes 4194320 | tf_op jit(solution)/shard_map/psum | solution.py:63
  436.6 6.6 multiply_reduce_fusion.1
  445.1 1.9 fusion.18
  453.5 2.3 select_subtract_fusion.9
  466.9 2.0 fusion.33
  474.6 10.6 %fusion = bf16[4096,512,1]{1,0,2:T(8,128)(2,1)} fusion(bf16[4096,512]{1,0:T(8,128)(2,1)} %all-reduce.3.cloned.1.call-done, f32[512,512]{1,0:T(8,128)S(1)} %fusion.34, f32[]{:T(128)S(6)} %sqrt.13), kind=kOutput, calls=%fused_computation.5 | convolution fusion | flops 12889096192 | bytes 9437188 | tf_op jit(solution)/shard_map/dot_general | solution.py:67
  485.2 29.6 %bitcast_convert_fusion = bf16[4096,512]{1,0:T(8,128)(2,1)} fusion(bf16[24,48,4096]{2,1,0:T(8,128)(2,1)} %squeeze.6, bf16[4096,512,1]{1,0,2:T(8,128)(2,1)} %fusion), kind=kOutput, calls=%fused_computation.1 | convolution fusion | flops 9666363392 | bytes 17825792 | tf_op jit(solution)/shard_map/kcd,kcr->dr/dot_general | solution.py:60
  514.9 111.5 %all-reduce.5.cloned.1.call-done = bf16[4096,512]{1,0:T(8,128)(2,1)} async-done(((bf16[4096,512]{1,0:T(8,128)(2,1)}), bf16[4096,512]{1,0:T(8,128)(2,1)}) %all-reduce.5.cloned.1.call-update) | async-done | bytes 4194320 | tf_op jit(solution)/shard_map/psum | solution.py:63
  626.3 6.6 multiply_reduce_fusion
  643.2 2.0 select_subtract_fusion.3
  656.3 2.1 fusion.42
  664.1 8.6 %multiply_convert_fusion = bf16[4096,512]{1,0:T(8,128)(2,1)S(1)} fusion(bf16[4096,512]{1,0:T(8,128)(2,1)} %all-reduce.5.cloned.1.call-done, f32[512,512]{1,0:T(8,128)S(1)} %fusion.43, f32[]{:T(128)S(6)} %sqrt.15), kind=kOutput, calls=%fused_computation.3 | convolution fusion | flops 12889096192 | bytes 9437188 | tf_op jit(solution)/shard_map/dot_general | solution.py:67
  672.7 8.7 %fusion.13 = bf16[1,24,48,512]{3,2,1,0:T(8,128)(2,1)} fusion(bf16[24,48,4096]{2,1,0:T(8,128)(2,1)} %squeeze.6, bf16[4096,512]{1,0:T(8,128)(2,1)S(1)} %multiply_convert_fusion), kind=kOutput, calls=%fused_computation.25 | convolution fusion | flops 4832428032 | bytes 14811136 | tf_op jit(solution)/shard_map/kcd,dr->kcr/dot_general | solution.py:69
  (44 shorter events, 51.8 us)
Async XLA Ops:
  19.8 9.8 %copy-start = (s32[64,1]{0,1:T(1,128)S(1)}, s32[64,1]{0,1:T(1,128)}, u32[]{:S(2)}) copy-start(s32[64,1]{0,1:T(1,128)} %param.6) | copy-start | bytes 772
  19.8 87.6 %all-to-all-start = ((bf16[2,1536,1024]{2,0,1:T(2,128)(2,1)}), bf16[2,1536,1024]{2,0,1:T(2,128)(2,1)}, u32[]{:S(2)}, u32[]{:S(2)}) async-start(bf16[2,1536,1024]{2,0,1:T(2,128)(2,1)} %copy.9), calls=%async_computation | async-start | bytes 12582912 | tf_op jit(solution)/shard_map/all_to_all | solution.py:43
  29.4 407.2 %all-reduce.3.cloned.1.call-start = ((), (), s32[]{:S(2)}) async-start(), calls=%async_computation.2 | async-start | bytes 8388608 | tf_op jit(solution)/shard_map/psum | solution.py:63
  112.4 6.5 copy-start.1
  315.9 310.4 %all-reduce.5.cloned.1.call-start = ((), (), s32[]{:S(2)}) async-start(), calls=%async_computation.3 | async-start | bytes 8388608 | tf_op jit(solution)/shard_map/psum | solution.py:63
Sparse Core Ops, SparseCore 0:
  316.0 120.5 all-reduce.2
  515.0 111.3 all-reduce.4
where the time goes:
time: 700 us; the launch traced here: 689 us
  waiting for transfers between devices  309 us (44%)
  matrix products  170 us (24%)
  blocking collectives  107 us (15%)
  local copies, waits for them, and re-layouts  76.6 us (11%)
  between operations  16.3 us (2%)
  starting transfers between devices  9.87 us (1%)
    psum x2, waiting for transfers between devices, body(): lax.psum(partial_value.astype(jnp.bfloat16), 'mem').astype(jnp.float32)  232 us
    all_to_all x1, blocking collectives, body(): lax.all_to_all(outgoing, 'grp', split_axis=0, concat_axis=3, tiled=True)  107 us
    all_to_all x1, waiting for transfers between devices, body(): lax.all_to_all(weights, 'mem', split_axis=1, concat_axis=0, tiled=True)  77.5 us
    dot_general x2, matrix products, body(): jnp.einsum('kcd,kcr->dr', regrouped, projected, preferred_element_type=jn...  58.9 us
    unnamed x7, local copies, waits for them, and re-layouts  32.9 us
    all_to_all x1, local copies, waits for them, and re-layouts, body(): lax.all_to_all(outgoing, 'grp', split_axis=0, concat_axis=3, tiled=True)  21.9 us
    dot_general x12, matrix products, inverse_root(): jnp.dot(root, scaled, precision=lax.Precision.HIGHEST)  21.3 us
    dot_general x12, matrix products, inverse_root(): root = jnp.dot(factor, root, precision=lax.Precision.HIGHEST)  20.4 us
  transfers between devices with their start and end apart: 3, of which 3 were waited for; matrix products, arithmetic and copies ran while one was open for 0% of the time, Pallas kernels for 0%

commit v1 on v0

v1 whole, which is shorter than its diff:
```python
import jax
import jax.numpy as jnp
from jax import lax
from jax.experimental import pallas as pl
from jax.experimental.pallas import tpu as pltpu
from jax.sharding import PartitionSpec as P

ITERS = 2
NS_STEPS = 6
MESH = pl.DeviceIdType.MESH
F32 = jnp.float32
BF16 = jnp.bfloat16
ROW = 16
VMEM_LIMIT = 60 * 1024 * 1024


def remote(src, dst, send, recv, device):
    return pltpu.make_async_remote_copy(
        src_ref=src, dst_ref=dst, send_sem=send, recv_sem=recv, device_id=device, device_id_type=MESH
    )


def greet(peers):
    barrier = pltpu.get_barrier_semaphore()
    for peer in peers:
        pl.semaphore_signal(barrier, inc=1, device_id=peer, device_id_type=MESH)
    pl.semaphore_wait(barrier, len(peers))


def slot_sources(stored_order, assignment, groups, capacity):
    assign = assignment[:, 0]
    experts = assign.shape[0]
    ids = jnp.arange(experts, dtype=jnp.int32)
    same = (assign[None, :] == assign[:, None]) & (ids[None, :] < ids[:, None])
    slot = assign * capacity + jnp.sum(same.astype(jnp.int32), axis=1)
    held = (stored_order[:, None] == ids[None, :]).astype(jnp.int32)
    slot_of_position = jnp.sum(held * slot[None, :], axis=1)
    slots = jnp.arange(groups * capacity, dtype=jnp.int32)
    hit = (slot_of_position[None, :] == slots[:, None]).astype(jnp.int32)
    return experts + jnp.sum(hit * (ids - experts)[None, :], axis=1)


def regroup(weights, sources, groups, members, capacity):
    held, rows, columns = weights.shape
    experts = held * members
    share = rows // members
    row_parts, col_parts = share // ROW, 2
    width = columns // col_parts
    chunks = [(r, h) for r in range(row_parts) for h in range(col_parts)]
    total = len(chunks)

    def kernel(sources_ref, w_ref, out_ref, packed, own_sem, a_send, a_recv, b_send, b_recv, *landed):
        g, m = lax.axis_index("grp"), lax.axis_index("mem")
        others = [(g, m ^ (k ^ (k >> 1))) for k in range(1, members)]
        across = [(lax.rem(g + k, groups), m) for k in range(1, groups)]
        greet(others + across)

        def piece(ci, member):
            r, h = chunks[ci]
            return w_ref.at[:, pl.ds(share * member + ROW * r, ROW), pl.ds(width * h, width)]

        def own(ci):
            return pltpu.make_async_copy(
                piece(ci, m), landed[ci].at[pl.ds(held * m, held)], own_sem.at[ci]
            )

        for ci in range(total):
            own(ci).start()
            for dev in others:
                remote(
                    piece(ci, dev[1]), landed[ci].at[pl.ds(held * m, held)], a_send.at[ci], a_recv.at[ci], dev
                ).start()
            landed[ci][experts] = jnp.zeros((ROW, width), BF16)

        def target(ci, source_group):
            r, h = chunks[ci]
            return out_ref.at[r, :, pl.ds(columns * source_group + width * h, width)]

        def keep(ci):
            return pltpu.make_async_copy(packed.at[ci, g], target(ci, g), own_sem.at[total + ci])

        def cross(ci, k):
            dev = across[k - 1]
            return remote(packed.at[ci, dev[0]], target(ci, g), b_send.at[ci, k], b_recv.at[ci, k], dev)

        for ci in range(total):
            own(ci).wait()
            arrivals = landed[ci].at[pl.ds(0, experts - held)]
            pltpu.make_async_copy(arrivals, arrivals, a_recv.at[ci]).wait()

            def pack(k, carry, ci=ci):
                for group in range(groups):
                    packed[ci, group, pl.ds(pl.multiple_of(k * ROW, ROW), ROW), :] = landed[ci][
                        sources_ref[group * capacity + k]
                    ]
                return carry

            lax.fori_loop(0, capacity, pack, 0)
            for k in range(1, groups):
                cross(ci, k).start()
            keep(ci).start()
        for ci in range(total):
            keep(ci).wait()
            for k in range(1, groups):
                cross(ci, k).wait()
            sent = landed[ci].at[pl.ds(0, experts - held)]
            pltpu.make_async_copy(sent, sent, a_send.at[ci]).wait()

    return pl.pallas_call(
        kernel,
        out_shape=jax.ShapeDtypeStruct((row_parts, capacity * ROW, groups * columns), BF16),
        in_specs=[pl.BlockSpec(memory_space=pltpu.SMEM), pl.BlockSpec(memory_space=pl.ANY)],
        out_specs=pl.BlockSpec(memory_space=pl.ANY),
        scratch_shapes=[
            pltpu.VMEM((total, groups, capacity * ROW, width), BF16),
            pltpu.SemaphoreType.DMA((2 * total,)),
            pltpu.SemaphoreType.DMA((total,)),
            pltpu.SemaphoreType.DMA((total,)),
            pltpu.SemaphoreType.DMA((total, groups)),
            pltpu.SemaphoreType.DMA((total, groups)),
        ]
        + [pltpu.VMEM((experts + 1, ROW, width), BF16)] * total,
        compiler_params=pltpu.CompilerParams(
            collective_id=0, has_side_effects=True, vmem_limit_bytes=VMEM_LIMIT
        ),
        cost_estimate=pl.CostEstimate(flops=0, bytes_accessed=32 << 20, transcendentals=0),
        name="regroup",
    )(sources, weights)


NN = (((1,), (0,)), ((), ()))
NT = (((1,), (1,)), ((), ()))


def mm(a, b, dims=NN):
    return lax.dot_general(a, b, dims, preferred_element_type=F32)


def split(x):
    high = x.astype(BF16)
    return high, (x - high.astype(F32)).astype(BF16)


def mm3(a, b, dims=NN):
    return mm(a[0], b[0], dims) + (mm(a[0], b[1], dims) + mm(a[1], b[0], dims))


def eye(n):
    return (lax.broadcasted_iota(jnp.int32, (n, n), 0) == lax.broadcasted_iota(jnp.int32, (n, n), 1)).astype(F32)


def iterate(regrouped, start, capacity):
    parts, part_rows, depth = regrouped.shape
    rank = start.shape[1]
    rows = parts * part_rows
    chunk = depth // 8
    half = rank // 2
    quarter = half // 4

    def kernel(
        w_ref, b_ref, basis_ref, coef_ref,
        proj, proj_t, full, out1, in1, sum1, in2, sum2, in3, root_hi, root_lo, scale_ref,
        send, recv,
    ):
        g, m = lax.axis_index("grp"), lax.axis_index("mem")
        x, z, c = m // 8, lax.rem(m // 2, 4), lax.rem(m, 2)
        sib = 1 - c
        member = lambda xx, zz, cc: (g, 8 * xx + 2 * zz + cc)
        turn = lambda v, o: lax.rem(v + o, 4)
        sibling = member(x, z, sib)
        xs = [None] + [member(turn(x, o), z, c) for o in (1, 2, 3)]
        zs = [None] + [member(x, turn(z, o), c) for o in (1, 2, 3)]
        first, second = (xs, zs), (zs, xs)
        place, other = (x, z), (z, x)
        greet([sibling] + xs[1:] + zs[1:])

        def copy(stage, h, o, src, dst, dev):
            return remote(src, dst, send.at[stage, h, o], recv.at[stage, h, o], dev)

        HALVES = (0, 1)
        steps = [(o, h) for o in (1, 2, 3, 0) for h in HALVES]

        for r in range(parts):
            proj[r * part_rows : (r + 1) * part_rows, :] = mm(w_ref[r], b_ref[...])
        root_hi[...] = eye(rank).astype(BF16)
        root_lo[...] = jnp.zeros((rank, rank), BF16)
        scale_ref[0] = jnp.float32(1.0)

        def columns_of(which):
            return pl.ds(pl.multiple_of(which * chunk, chunk), chunk)

        def image_piece(core, q, h):
            total = None
            for r in range(parts):
                term = mm(
                    proj_t[h * half : (h + 1) * half, r * part_rows : (r + 1) * part_rows],
                    w_ref[r, :, columns_of(core * 4 + q)],
                )
                total = term if total is None else total + term
            return total

        def sweep(it, carry):
            root = (root_hi[...], root_lo[...])
            for r in range(parts):
                at = slice(r * part_rows, (r + 1) * part_rows)
                proj_t[:, at] = (mm3(root, split(proj[at, :]), NT) * scale_ref[0]).astype(BF16)

            ship1 = {}
            for o, h in steps:
                out1[h, o] = image_piece(sib, turn(place[h], o), h).astype(BF16)
                ship1[o, h] = copy(0, h, o, out1.at[h, o], in1.at[h, o], sibling)
                ship1[o, h].start()
            ship2 = {}
            for o, h in steps:
                mine = image_piece(c, turn(place[h], o), h)
                ship1[o, h].wait_recv()
                sum1[h, o] = (mine + in1[h, o].astype(F32)).astype(BF16)
                if o:
                    ship2[o, h] = copy(1, h, o, sum1.at[h, o], in2.at[h, o], first[h][o])
                    ship2[o, h].start()
            ship3 = {}
            for h in HALVES:
                for o in (1, 2, 3):
                    ship2[o, h].wait_recv()
                sum2[h] = (
                    (sum1[h, 0].astype(F32) + in2[h, 1].astype(F32))
                    + (in2[h, 2].astype(F32) + in2[h, 3].astype(F32))
                ).astype(BF16)
                for o in (1, 2, 3):
                    rows_there = pl.ds(pl.multiple_of(turn(other[h], o) * quarter, quarter), quarter)
                    ship3[o, h] = copy(2, h, o, sum2.at[h, rows_there], in3.at[h, o], second[h][o])
                    ship3[o, h].start()
            ship4, ship5, ship6 = {}, {}, {}
            for h in HALVES:
                for o in (1, 2, 3):
                    ship3[o, h].wait_recv()
                mine_rows = pl.ds(pl.multiple_of(other[h] * quarter, quarter), quarter)
                here = pl.ds(pl.multiple_of(h * half + other[h] * quarter, quarter), quarter)
                total = (sum2[h, mine_rows].astype(F32) + in3[h, 1].astype(F32)) + (
                    in3[h, 2].astype(F32) + in3[h, 3].astype(F32)
                )
                spot = full.at[c * 4 + place[h], here]
                full[c * 4 + place[h], here, :] = total.astype(BF16)
                for o in (1, 2, 3):
                    ship4[o, h] = copy(3, h, o, spot, spot, second[h][o])
                    ship4[o, h].start()

            def spot_of(core, q, h):
                return full.at[core * 4 + q, pl.ds(h * half, half)]

            def absorb(core, q, h, start):
                cols = slice(h * half, (h + 1) * half)
                block = full[core * 4 + q, h * half : (h + 1) * half, :]
                for r in range(parts):
                    at = slice(r * part_rows, (r + 1) * part_rows)
                    term = mm(w_ref[r, :, columns_of(core * 4 + q)], block, NT)
                    if start:
                        proj[at, cols] = term
                    else:
                        proj[at, cols] += term

            for h in HALVES:
                for o in (1, 2, 3):
                    ship4[o, h].wait_recv()
                spot = spot_of(c, place[h], h)
                for o in (1, 2, 3):
                    ship5[o, h] = copy(4, h, o, spot, spot, first[h][o])
                    ship5[o, h].start()
                ship6[0, h] = copy(5, h, 0, spot, spot, sibling)
                ship6[0, h].start()
            for h in HALVES:
                absorb(c, place[h], h, True)
            for h in HALVES:
                ship6[0, h].wait_recv()
                absorb(sib, place[h], h, False)
            for o in (1, 3, 2):
                for h in HALVES:
                    q = turn(place[h], 4 - o)
                    ship5[o, h].wait_recv()
                    spot = spot_of(c, q, h)
                    ship6[o, h] = copy(5, h, o, spot, spot, sibling)
                    ship6[o, h].start()
                for h in HALVES:
                    absorb(c, turn(place[h], 4 - o), h, False)
                for h in HALVES:
                    ship6[o, h].wait_recv()
                    absorb(sib, turn(place[h], 4 - o), h, False)

            gram = None
            for d in range(8):
                term = mm(full[d], full[d], NT)
                gram = term if gram is None else gram + term
            frob = jnp.sqrt(jnp.sum(gram * gram)) + 1e-06
            scaled = split(gram / frob)
            ident = eye(rank)
            factor = split(1.5 * ident - 0.5 * (scaled[0].astype(F32) + scaled[1].astype(F32)))
            root = factor
            for inner in range(1, NS_STEPS):
                scaled = split(mm3(scaled, factor))
                factor = split(1.5 * ident - 0.5 * mm3(root, scaled))
                root = split(mm3(factor, root))
            root_hi[...] = root[0]
            root_lo[...] = root[1]
            scale_ref[0] = jnp.sqrt(jnp.float32(depth) / frob)

            for o, h in steps:
                ship1[o, h].wait_send()
                ship6[o, h].wait_send()
                if o:
                    for ship in (ship2, ship3, ship4, ship5):
                        ship[o, h].wait_send()
            return carry

        lax.fori_loop(0, ITERS, sweep, 0)

        root = (root_hi[...], root_lo[...])
        scale = scale_ref[0]
        for r in range(parts):
            value = mm3(split(proj[r * part_rows : (r + 1) * part_rows, :]), root) * scale
            coef_ref[:, r * ROW : (r + 1) * ROW, :] = value.astype(BF16).reshape(capacity, ROW, rank)
        block = full[m // 4, :, pl.ds(pl.multiple_of(lax.rem(m, 4) * 128, 128), 128)]
        turned = mm(eye(128).astype(BF16), block, NT).astype(BF16)
        basis_ref[...] = ((mm(turned, root[0]) + mm(turned, root[1])) * scale).astype(BF16)

    return pl.pallas_call(
        kernel,
        out_shape=(
            jax.ShapeDtypeStruct((128, rank), BF16),
            jax.ShapeDtypeStruct((capacity, parts * ROW, rank), BF16),
        ),
        in_specs=[pl.BlockSpec(memory_space=pltpu.VMEM)] * 2,
        out_specs=(pl.BlockSpec(memory_space=pltpu.VMEM),) * 2,
        scratch_shapes=[
            pltpu.VMEM((rows, rank), F32),
            pltpu.VMEM((rank, rows), BF16),
            pltpu.VMEM((8, rank, chunk), BF16),
            pltpu.VMEM((2, 4, half, chunk), BF16),
            pltpu.VMEM((2, 4, half, chunk), BF16),
            pltpu.VMEM((2, 4, half, chunk), BF16),
            pltpu.VMEM((2, 4, half, chunk), BF16),
            pltpu.VMEM((2, half, chunk), BF16),
            pltpu.VMEM((2, 4, quarter, chunk), BF16),
            pltpu.VMEM((rank, rank), BF16),
            pltpu.VMEM((rank, rank), BF16),
            pltpu.SMEM((1,), F32),
            pltpu.SemaphoreType.DMA((6, 2, 4)),
            pltpu.SemaphoreType.DMA((6, 2, 4)),
        ],
        compiler_params=pltpu.CompilerParams(
            collective_id=1, has_side_effects=True, vmem_limit_bytes=VMEM_LIMIT
        ),
        cost_estimate=pl.CostEstimate(flops=40 << 30, bytes_accessed=32 << 20, transcendentals=0),
        name="iterate",
    )(regrouped, start)


def body(weights, stored_order, assignment, init_basis):
    groups, members = lax.axis_size("grp"), lax.axis_size("mem")
    experts = weights.shape[0] * members
    capacity = experts // groups + experts // (2 * groups)
    sources = slot_sources(stored_order, assignment, groups, capacity)
    regrouped = regroup(weights, sources, groups, members, capacity)
    basis, coefficients = iterate(regrouped, init_basis[0], capacity)
    return (basis[None], coefficients[None])


def solution(mesh):
    return jax.shard_map(
        body,
        mesh=mesh,
        in_specs=(P("mem", None, "grp"), P(), P(), P("grp", None, None)),
        out_specs=(P("grp", "mem", None), P("grp", None, "mem", None)),
        check_vma=False,
    )
```

time: 700 us -> 291 us (0.42); the launches traced: 689 us -> 291 us
  waiting for transfers between devices: 309 us -> 0 us
  Pallas kernels: 0 us -> 283 us
  matrix products: 170 us -> 0 us
  blocking collectives: 107 us -> 0 us
  local copies, waits for them, and re-layouts: 76.6 us -> 3.93 us
  between operations: 16.3 us -> 0.66 us
  starting transfers between devices: 9.87 us -> 0 us
    pallas_call x0 -> x2, Pallas kernels: none -> 283 us  [the longest x1 157 us: iterate(): pl.pallas_call(kernel, out_shape=(jax.ShapeDtypeStruct((128, rank), BF16)...]
    psum x2 -> x0, waiting for transfers between devices: 232 us -> none  [body(): lax.psum(partial_value.astype(jnp.bfloat16), 'mem').astype(jnp.float32)]
    dot_general x42 -> x0, matrix products: 170 us -> none  [the longest x2 58.9 us: body(): jnp.einsum('kcd,kcr->dr', regrouped, projected, preferred_element_type=jn...]
    all_to_all x1 -> x0, blocking collectives: 107 us -> none  [body(): lax.all_to_all(outgoing, 'grp', split_axis=0, concat_axis=3, tiled=True)]
    all_to_all x1 -> x0, waiting for transfers between devices: 77.5 us -> none  [body(): lax.all_to_all(weights, 'mem', split_axis=1, concat_axis=0, tiled=True)]
    unnamed x7 -> x2, local copies, waits for them, and re-layouts: 32.9 us -> 3.93 us
    all_to_all x2 -> x0, local copies, waits for them, and re-layouts: 26.9 us -> none  [the longest x1 21.9 us: body(): lax.all_to_all(outgoing, 'grp', split_axis=0, concat_axis=3, tiled=True)]
    squeeze x1 -> x0, local copies, waits for them, and re-layouts: 16.1 us -> none  [body(): regrouped = arrived[0]]
  transfers between devices with their start and end apart: 3 -> 0, of which waited for: 3 -> 0; matrix products, arithmetic and copies ran while one was open for 0% -> 0% of each run, Pallas kernels for 0% -> 0%
where the time goes in v1:
time: 291 us
  Pallas kernels  283 us (97%)
  local copies, waits for them, and re-layouts  3.93 us (1%)
  other arithmetic  3.03 us (1%)
    pallas_call x1, Pallas kernels, iterate(): pl.pallas_call(kernel, out_shape=(jax.ShapeDtypeStruct((128, rank), BF16)...  157 us
    pallas_call x1, Pallas kernels, regroup(): pl.pallas_call(kernel, out_shape=jax.ShapeDtypeStruct((row_parts, capacit...  126 us

profile of v1, /device:TPU:1, one launch (start us, length us, event | category | flops | bytes accessed | tf_op | source)
XLA Modules:
  0.0 290.8 jit_solution(8259992867512477562)
XLA Ops:
  0.6 0.9 convert_reduce_fusion
  1.5 0.7 multiply_add_fusion
  2.2 0.8 select_reduce_fusion.1
  3.1 0.1 select_reduce_fusion
  3.2 0.5 broadcast_add_fusion.sources_ref
  3.7 125.8 %regroup.1.w_ref = bf16[3,384,4096]{2,1,0:T(8,128)(2,1)} custom-call(s32[96]{0:T(128)} %broadcast_add_fusion.sources_ref, bf16[2,1536,1024]{2,1,0:T(8,128)(2,1)} %w_ref.1), custom_call_target="tpu_custom_call" | custom-call | bytes 33554432 | tf_op jit(solution)/shard_map/regroup/pallas_call | solution.py:109
  129.5 157.3 %iterate.1 = (bf16[128,512]{1,0:T(8,128)(2,1)}, bf16[24,48,512]{2,1,0:T(8,128)(2,1)}) custom-call(bf16[3,384,4096]{2,1,0:T(8,128)(2,1)} %regroup.1.w_ref, bf16[4096,512]{1,0:T(8,128)(2,1)} %bitcast.7), custom_call_target="tpu_custom_call" | custom-call | flops 42949672960 | bytes 33554432 | tf_op jit(solution)/shard_map/iterate/pallas_call | solution.py:325
  286.9 1.6 copy.8
  288.4 2.4 copy.9
  (1 shorter events, 0.0 us)

commit v2 on v1

v2 whole, which is shorter than its diff:
```python
import jax
import jax.numpy as jnp
from jax import lax
from jax.experimental import pallas as pl
from jax.experimental.pallas import tpu as pltpu
from jax.sharding import PartitionSpec as P

ITERS = 2
NS_STEPS = 6
MESH = pl.DeviceIdType.MESH
F32 = jnp.float32
BF16 = jnp.bfloat16
ROW = 16
VMEM_LIMIT = 60 * 1024 * 1024


def remote(src, dst, send, recv, device):
    return pltpu.make_async_remote_copy(
        src_ref=src, dst_ref=dst, send_sem=send, recv_sem=recv, device_id=device, device_id_type=MESH
    )


def greet(peers):
    barrier = pltpu.get_barrier_semaphore()
    for peer in peers:
        pl.semaphore_signal(barrier, inc=1, device_id=peer, device_id_type=MESH)
    pl.semaphore_wait(barrier, len(peers))


def slot_sources(stored_order, assignment, groups, capacity):
    assign = assignment[:, 0]
    experts = assign.shape[0]
    ids = jnp.arange(experts, dtype=jnp.int32)
    same = (assign[None, :] == assign[:, None]) & (ids[None, :] < ids[:, None])
    slot = assign * capacity + jnp.sum(same.astype(jnp.int32), axis=1)
    held = (stored_order[:, None] == ids[None, :]).astype(jnp.int32)
    slot_of_position = jnp.sum(held * slot[None, :], axis=1)
    slots = jnp.arange(groups * capacity, dtype=jnp.int32)
    hit = (slot_of_position[None, :] == slots[:, None]).astype(jnp.int32)
    return experts + jnp.sum(hit * (ids - experts)[None, :], axis=1)


NN = (((1,), (0,)), ((), ()))
NT = (((1,), (1,)), ((), ()))


def mm(a, b, dims=NN):
    return lax.dot_general(a, b, dims, preferred_element_type=F32)


def split(x):
    high = x.astype(BF16)
    return high, (x - high.astype(F32)).astype(BF16)


def mm3(a, b, dims=NN):
    return mm(a[0], b[0], dims) + (mm(a[0], b[1], dims) + mm(a[1], b[0], dims))


def eye(n):
    return (lax.broadcasted_iota(jnp.int32, (n, n), 0) == lax.broadcasted_iota(jnp.int32, (n, n), 1)).astype(F32)


def inverse_root(gram, frob):
    ident = eye(gram.shape[0])
    scaled = gram / frob
    gap = (0.5 * (ident - scaled)).astype(BF16)
    halves = split(scaled)
    scaled = scaled + (mm(halves[0], gap) + mm(halves[1], gap))
    root = ident + gap.astype(F32)
    for inner in range(1, NS_STEPS):
        upper, lower = split(root), split(scaled)
        gap = (0.5 * (ident - mm3(upper, lower))).astype(BF16)
        root = root + (mm(gap, upper[0]) + mm(gap, upper[1]))
        if inner < NS_STEPS - 1:
            scaled = scaled + (mm(lower[0], gap) + mm(lower[1], gap))
    return split(root)


CHUNKS = [(0, 0, 256), (0, 256, 256), (0, 512, 512), (1, 0, 512), (1, 512, 512), (2, 0, 512), (2, 512, 256), (2, 768, 256)]
AHEAD = 3
ORDER = (2, 1, 3)
LAG = 3
AORDER = (1, 3, 2)


def fit(weights, sources, start, groups, members, capacity):
    held, rows_all, columns = weights.shape
    experts = held * members
    share = rows_all // members
    parts = share // ROW
    part_rows = capacity * ROW
    total = len(CHUNKS)
    depth, rank = start.shape
    rows = parts * part_rows
    chunk = depth // 8
    half = rank // 2
    quarter = half // 4

    def kernel(
        sources_ref, weights_ref, start_ref, basis_ref, coef_ref,
        w_ref, b_ref, proj, proj_t, full, out1, in1, sum1, in2, sum2, in3, root_hi, root_lo, gram_ref, scale_ref,
        start_sem, own_sem, keep_sem, a_send, a_recv, b_send, b_recv, send, recv, *buffers,
    ):
        landed, packed = buffers[:total], buffers[total:]
        g, m = lax.axis_index("grp"), lax.axis_index("mem")
        x, z, c = m // 8, lax.rem(m // 2, 4), lax.rem(m, 2)
        sib = 1 - c
        member = lambda xx, zz, cc: (g, 8 * xx + 2 * zz + cc)
        turn = lambda v, o: lax.rem(v + o, 4)
        others = [(g, m ^ (k ^ (k >> 1))) for k in range(1, members)]
        across = [(lax.rem(g + k, groups), m) for k in range(1, groups)]
        load_start = pltpu.make_async_copy(start_ref, b_ref, start_sem)
        load_start.start()
        greet(others + across)

        def piece(ci, who):
            r, c0, width = CHUNKS[ci]
            return weights_ref.at[:, pl.ds(share * who + ROW * r, ROW), pl.ds(c0, width)]

        def own(ci):
            return pltpu.make_async_copy(piece(ci, m), landed[ci].at[pl.ds(held * m, held)], own_sem.at[ci])

        def launch(ci):
            own(ci).start()
            for dev in others:
                remote(
                    piece(ci, dev[1]), landed[ci].at[pl.ds(held * m, held)], a_send.at[ci], a_recv.at[ci], dev
                ).start()
            landed[ci][experts] = jnp.zeros((ROW, CHUNKS[ci][2]), BF16)

        def target(ci, source_group):
            r, c0, width = CHUNKS[ci]
            return w_ref.at[r, :, pl.ds(pl.multiple_of(columns * source_group + c0, 128), width)]

        def keep(ci):
            return pltpu.make_async_copy(packed[ci].at[g], target(ci, g), keep_sem.at[ci])

        def cross(ci, k):
            dev = across[k - 1]
            return remote(packed[ci].at[dev[0]], target(ci, g), b_send.at[ci, k], b_recv.at[ci, k], dev)

        for ci in range(min(AHEAD, total)):
            launch(ci)
        for ci in range(total):
            own(ci).wait()
            arrivals = landed[ci].at[pl.ds(0, experts - held)]
            pltpu.make_async_copy(arrivals, arrivals, a_recv.at[ci]).wait()

            def pack(k, carry, ci=ci):
                for group in range(groups):
                    packed[ci][group, pl.ds(pl.multiple_of(k * ROW, ROW), ROW), :] = landed[ci][
                        sources_ref[group * capacity + k]
                    ]
                return carry

            lax.fori_loop(0, capacity, pack, 0)
            for k in range(1, groups):
                cross(ci, k).start()
            keep(ci).start()
            if ci + AHEAD < total:
                launch(ci + AHEAD)

        load_start.wait()
        proj[...] = jnp.zeros_like(proj)
        ident = eye(rank).astype(BF16)
        for ci in range(total):
            keep(ci).wait()
            for k in range(1, groups):
                cross(ci, k).wait()
            r, c0, width = CHUNKS[ci]
            at = slice(r * part_rows, (r + 1) * part_rows)
            term = None
            for group in range(groups):
                cols = slice(columns * group + c0, columns * group + c0 + width)
                more = mm(w_ref[r, :, cols], b_ref[cols, :])
                term = more if term is None else term + more
            proj[at, :] += term
            if ci + 1 == total or CHUNKS[ci + 1][0] != r:
                proj_t[:, at] = mm(ident, proj[at, :].astype(BF16), NT).astype(BF16)

        sibling = member(x, z, sib)
        xs = [None] + [member(turn(x, o), z, c) for o in (1, 2, 3)]
        zs = [None] + [member(x, turn(z, o), c) for o in (1, 2, 3)]
        first, second = (xs, zs), (zs, xs)
        place, other = (x, z), (z, x)

        def copy(stage, h, o, src, dst, dev):
            return remote(src, dst, send.at[stage, h, o], recv.at[stage, h, o], dev)

        HALVES = (0, 1)
        steps = [(o, h) for o in ORDER + (0,) for h in HALVES]

        def columns_of(which):
            return pl.ds(pl.multiple_of(which * chunk, chunk), chunk)

        def image_piece(core, q, h):
            total = None
            for r in range(parts):
                term = mm(
                    proj_t[h * half : (h + 1) * half, r * part_rows : (r + 1) * part_rows],
                    w_ref[r, :, columns_of(core * 4 + q)],
                )
                total = term if total is None else total + term
            return total

        def sweep(it, carry):
            ship1, ship2, ship3, ship4, ship5, ship6 = {}, {}, {}, {}, {}, {}

            def give(o, h):
                out1[h, o] = image_piece(sib, turn(place[h], o), h).astype(BF16)
                ship1[o, h] = copy(0, h, o, out1.at[h, o], in1.at[h, o], sibling)
                ship1[o, h].start()

            def take(o, h):
                mine = image_piece(c, turn(place[h], o), h)
                ship1[o, h].wait_recv()
                sum1[h, o] = (mine + in1[h, o].astype(F32)).astype(BF16)
                if o:
                    ship2[o, h] = copy(1, h, o, sum1.at[h, o], in2.at[h, o], first[h][o])
                    ship2[o, h].start()

            for i in range(len(steps) + LAG):
                if i < len(steps):
                    give(*steps[i])
                if i >= LAG:
                    take(*steps[i - LAG])
            for h in HALVES:
                for o in (1, 2, 3):
                    ship2[o, h].wait_recv()
                sum2[h] = (
                    (sum1[h, 0].astype(F32) + in2[h, 1].astype(F32))
                    + (in2[h, 2].astype(F32) + in2[h, 3].astype(F32))
                ).astype(BF16)
                for o in ORDER:
                    rows_there = pl.ds(pl.multiple_of(turn(other[h], o) * quarter, quarter), quarter)
                    ship3[o, h] = copy(2, h, o, sum2.at[h, rows_there], in3.at[h, o], second[h][o])
                    ship3[o, h].start()
            for h in HALVES:
                for o in (1, 2, 3):
                    ship3[o, h].wait_recv()
                mine_rows = pl.ds(pl.multiple_of(other[h] * quarter, quarter), quarter)
                here = pl.ds(pl.multiple_of(h * half + other[h] * quarter, quarter), quarter)
                total = (sum2[h, mine_rows].astype(F32) + in3[h, 1].astype(F32)) + (
                    in3[h, 2].astype(F32) + in3[h, 3].astype(F32)
                )
                spot = full.at[c * 4 + place[h], here]
                full[c * 4 + place[h], here, :] = total.astype(BF16)
                for o in ORDER:
                    ship4[o, h] = copy(3, h, o, spot, spot, second[h][o])
                    ship4[o, h].start()

            def spot_of(core, q, h):
                return full.at[core * 4 + q, pl.ds(h * half, half)]

            def absorb(core, q, h, start):
                cols = slice(h * half, (h + 1) * half)
                block = full[core * 4 + q, h * half : (h + 1) * half, :]
                square = mm(block, block, NT)
                if start:
                    gram_ref[h] = square
                else:
                    gram_ref[h] += square
                for r in range(parts):
                    at = slice(r * part_rows, (r + 1) * part_rows)
                    term = mm(w_ref[r, :, columns_of(core * 4 + q)], block, NT)
                    if start:
                        proj[at, cols] = term
                    else:
                        proj[at, cols] += term

            for h in HALVES:
                for o in (1, 2, 3):
                    ship4[o, h].wait_recv()
                spot = spot_of(c, place[h], h)
                for o in ORDER:
                    ship5[o, h] = copy(4, h, o, spot, spot, first[h][o])
                    ship5[o, h].start()
                ship6[0, h] = copy(5, h, 0, spot, spot, sibling)
                ship6[0, h].start()
            for h in HALVES:
                absorb(c, place[h], h, True)
            for h in HALVES:
                ship6[0, h].wait_recv()
                absorb(sib, place[h], h, False)
            for o in AORDER:
                for h in HALVES:
                    q = turn(place[h], 4 - o)
                    ship5[o, h].wait_recv()
                    spot = spot_of(c, q, h)
                    ship6[o, h] = copy(5, h, o, spot, spot, sibling)
                    ship6[o, h].start()
                for h in HALVES:
                    absorb(c, turn(place[h], 4 - o), h, False)
                for h in HALVES:
                    ship6[o, h].wait_recv()
                    absorb(sib, turn(place[h], 4 - o), h, False)

            cross_gram = None
            for d in range(8):
                term = mm(full[d, 0:half, :], full[d, half:rank, :], NT)
                cross_gram = term if cross_gram is None else cross_gram + term
            gram = jnp.concatenate(
                [
                    jnp.concatenate([gram_ref[0], cross_gram], axis=1),
                    jnp.concatenate([cross_gram.T, gram_ref[1]], axis=1),
                ],
                axis=0,
            )
            frob = jnp.sqrt(jnp.sum(gram * gram)) + 1e-06
            root = inverse_root(gram, frob)
            scale = jnp.sqrt(jnp.float32(depth) / frob)
            root_hi[...] = root[0]
            root_lo[...] = root[1]
            scale_ref[0] = scale

            @pl.when(it + 1 < ITERS)
            def _():
                for r in range(parts):
                    at = slice(r * part_rows, (r + 1) * part_rows)
                    proj_t[:, at] = (mm3(root, split(proj[at, :]), NT) * scale).astype(BF16)

            for o, h in steps:
                ship1[o, h].wait_send()
                ship6[o, h].wait_send()
                if o:
                    for ship in (ship2, ship3, ship4, ship5):
                        ship[o, h].wait_send()
            return carry

        lax.fori_loop(0, ITERS, sweep, 0)

        root = (root_hi[...], root_lo[...])
        scale = scale_ref[0]
        for r in range(parts):
            value = mm3(split(proj[r * part_rows : (r + 1) * part_rows, :]), root) * scale
            coef_ref[:, r * ROW : (r + 1) * ROW, :] = value.astype(BF16).reshape(capacity, ROW, rank)
        block = full[m // 4, :, pl.ds(pl.multiple_of(lax.rem(m, 4) * 128, 128), 128)]
        turned = mm(eye(128).astype(BF16), block, NT).astype(BF16)
        basis_ref[...] = ((mm(turned, root[0]) + mm(turned, root[1])) * scale).astype(BF16)
        for ci in range(total):
            sent = landed[ci].at[pl.ds(0, experts - held)]
            pltpu.make_async_copy(sent, sent, a_send.at[ci]).wait()

    return pl.pallas_call(
        kernel,
        out_shape=(
            jax.ShapeDtypeStruct((128, rank), BF16),
            jax.ShapeDtypeStruct((capacity, parts * ROW, rank), BF16),
        ),
        in_specs=[pl.BlockSpec(memory_space=pltpu.SMEM)] + [pl.BlockSpec(memory_space=pl.ANY)] * 2,
        out_specs=(pl.BlockSpec(memory_space=pltpu.VMEM),) * 2,
        scratch_shapes=[
            pltpu.VMEM((parts, part_rows, depth), BF16),
            pltpu.VMEM((depth, rank), BF16),
            pltpu.VMEM((rows, rank), F32),
            pltpu.VMEM((rank, rows), BF16),
            pltpu.VMEM((8, rank, chunk), BF16),
            pltpu.VMEM((2, 4, half, chunk), BF16),
            pltpu.VMEM((2, 4, half, chunk), BF16),
            pltpu.VMEM((2, 4, half, chunk), BF16),
            pltpu.VMEM((2, 4, half, chunk), BF16),
            pltpu.VMEM((2, half, chunk), BF16),
            pltpu.VMEM((2, 4, quarter, chunk), BF16),
            pltpu.VMEM((rank, rank), BF16),
            pltpu.VMEM((rank, rank), BF16),
            pltpu.VMEM((2, half, half), F32),
            pltpu.SMEM((1,), F32),
            pltpu.SemaphoreType.DMA,
            pltpu.SemaphoreType.DMA((total,)),
            pltpu.SemaphoreType.DMA((total,)),
            pltpu.SemaphoreType.DMA((total,)),
            pltpu.SemaphoreType.DMA((total,)),
            pltpu.SemaphoreType.DMA((total, groups)),
            pltpu.SemaphoreType.DMA((total, groups)),
            pltpu.SemaphoreType.DMA((6, 2, 4)),
            pltpu.SemaphoreType.DMA((6, 2, 4)),
        ]
        + [pltpu.VMEM((experts + 1, ROW, width), BF16) for _, _, width in CHUNKS]
        + [pltpu.VMEM((groups, part_rows, width), BF16) for _, _, width in CHUNKS],
        compiler_params=pltpu.CompilerParams(
            collective_id=0, has_side_effects=True, vmem_limit_bytes=VMEM_LIMIT
        ),
        cost_estimate=pl.CostEstimate(flops=60 << 30, bytes_accessed=16 << 20, transcendentals=0),
        name="fit",
    )(sources, weights, start)


def body(weights, stored_order, assignment, init_basis):
    groups, members = lax.axis_size("grp"), lax.axis_size("mem")
    experts = weights.shape[0] * members
    capacity = experts // groups + experts // (2 * groups)
    sources = slot_sources(stored_order, assignment, groups, capacity)
    basis, coefficients = fit(weights, sources, init_basis[0], groups, members, capacity)
    return (basis[None], coefficients[None])


def solution(mesh):
    return jax.shard_map(
        body,
        mesh=mesh,
        in_specs=(P("mem", None, "grp"), P(), P(), P("grp", None, None)),
        out_specs=(P("grp", "mem", None), P("grp", None, "mem", None)),
        check_vma=False,
    )
```

time: 291 us -> 258 us (0.89)
  Pallas kernels: 283 us -> 250 us
    pallas_call x2 -> x1, Pallas kernels: 283 us -> 250 us  [fit(): pl.pallas_call(kernel, out_shape=(jax.ShapeDtypeStruct((128, rank), BF16)...]
where the time goes in v2:
time: 258 us; the launch traced here: 257 us
  Pallas kernels  250 us (97%)
  local copies, waits for them, and re-layouts  3.93 us (2%)
  other arithmetic  3.03 us (1%)
    pallas_call x1, Pallas kernels, fit(): pl.pallas_call(kernel, out_shape=(jax.ShapeDtypeStruct((128, rank), BF16)...  250 us

profile of v2, /device:TPU:1, one launch (start us, length us, event | category | flops | bytes accessed | tf_op | source)
XLA Modules:
  0.0 257.3 jit_solution(16356107526568684583)
XLA Ops:
  0.6 0.9 convert_reduce_fusion
  1.5 0.7 multiply_add_fusion
  2.2 0.8 select_reduce_fusion.1
  3.1 0.1 select_reduce_fusion
  3.2 0.5 broadcast_add_fusion.sources_ref
  3.7 249.6 %fit.1 = (bf16[128,512]{1,0:T(8,128)(2,1)}, bf16[24,48,512]{2,1,0:T(8,128)(2,1)}) custom-call(s32[96]{0:T(128)} %broadcast_add_fusion.sources_ref, bf16[2,1536,1024]{2,1,0:T(8,128)(2,1)} %weights_ref.1, bf16[4096,512]{1,0:T(8,128)(2,1)} %bitcast.7), custom_call_target="tpu_custom_call" | custom-call | flops 64424509440 | bytes 16777216 | tf_op jit(solution)/shard_map/fit/pallas_call | solution.py:345
  253.3 1.6 copy.8
  254.9 2.4 copy.9
  (1 shorter events, 0.0 us)

commit v3 on v2

--- a/solution.py
+++ b/solution.py
@@ -81,6 +81,7 @@
 AHEAD = 3
 ORDER = (2, 1, 3)
 LAG = 3
+CUTS = 2
 AORDER = (1, 3, 2)
 
 
@@ -93,7 +94,7 @@
     total = len(CHUNKS)
     depth, rank = start.shape
     rows = parts * part_rows
-    chunk = depth // 8
+    chunk = depth // 8 // CUTS
     half = rank // 2
     quarter = half // 4
 
@@ -131,7 +132,7 @@
 
         def target(ci, source_group):
             r, c0, width = CHUNKS[ci]
-            return w_ref.at[r, :, pl.ds(pl.multiple_of(columns * source_group + c0, 128), width)]
+            return w_ref.at[pl.ds(r * part_rows, part_rows), pl.ds(pl.multiple_of(columns * source_group + c0, 128), width)]
 
         def keep(ci):
             return pltpu.make_async_copy(packed[ci].at[g], target(ci, g), keep_sem.at[ci])
@@ -173,7 +174,7 @@
             term = None
             for group in range(groups):
                 cols = slice(columns * group + c0, columns * group + c0 + width)
-                more = mm(w_ref[r, :, cols], b_ref[cols, :])
+                more = mm(w_ref[at, cols], b_ref[cols, :])
                 term = more if term is None else term + more
             proj[at, :] += term
             if ci + 1 == total or CHUNKS[ci + 1][0] != r:
@@ -185,119 +186,139 @@
         first, second = (xs, zs), (zs, xs)
         place, other = (x, z), (z, x)
 
-        def copy(stage, h, o, src, dst, dev):
-            return remote(src, dst, send.at[stage, h, o], recv.at[stage, h, o], dev)
+        def copy(stage, h, u, o, src, dst, dev):
+            return remote(src, dst, send.at[stage, h, u, o], recv.at[stage, h, u, o], dev)
 
         HALVES = (0, 1)
-        steps = [(o, h) for o in ORDER + (0,) for h in HALVES]
-
-        def columns_of(which):
-            return pl.ds(pl.multiple_of(which * chunk, chunk), chunk)
-
-        def image_piece(core, q, h):
-            total = None
-            for r in range(parts):
-                term = mm(
-                    proj_t[h * half : (h + 1) * half, r * part_rows : (r + 1) * part_rows],
-                    w_ref[r, :, columns_of(core * 4 + q)],
-                )
-                total = term if total is None else total + term
-            return total
+        steps = [(u, o, h) for u in range(CUTS) for o in ORDER + (0,) for h in HALVES]
+
+        def index_of(core, q, u):
+            return (core * 4 + q) * CUTS + u
+
+        def columns_of(core, q, u):
+            return pl.ds(pl.multiple_of(index_of(core, q, u) * chunk, chunk), chunk)
+
+        def image_piece(core, q, u, h):
+            left = proj_t.at[pl.ds(h * half, half)]
+            cols = columns_of(core, q, u)
+            cut = rows // 256 * 256
+            return mm(left[:, 0:cut], w_ref[0:cut, cols]) + mm(left[:, cut:rows], w_ref[cut:rows, cols])
 
         def sweep(it, carry):
             ship1, ship2, ship3, ship4, ship5, ship6 = {}, {}, {}, {}, {}, {}
 
-            def give(o, h):
-                out1[h, o] = image_piece(sib, turn(place[h], o), h).astype(BF16)
-                ship1[o, h] = copy(0, h, o, out1.at[h, o], in1.at[h, o], sibling)
-                ship1[o, h].start()
-
-            def take(o, h):
-                mine = image_piece(c, turn(place[h], o), h)
-                ship1[o, h].wait_recv()
-                sum1[h, o] = (mine + in1[h, o].astype(F32)).astype(BF16)
+            def give(u, o, h):
+                out1[h, u, o] = image_piece(sib, turn(place[h], o), u, h).astype(BF16)
+                ship1[u, o, h] = copy(0, h, u, o, out1.at[h, u, o], in1.at[h, u, o], sibling)
+                ship1[u, o, h].start()
+
+            def take(u, o, h):
+                mine = image_piece(c, turn(place[h], o), u, h)
+                ship1[u, o, h].wait_recv()
+                sum1[h, u, o] = (mine + in1[h, u, o].astype(F32)).astype(BF16)
                 if o:
-                    ship2[o, h] = copy(1, h, o, sum1.at[h, o], in2.at[h, o], first[h][o])
-                    ship2[o, h].start()
+                    ship2[u, o, h] = copy(1, h, u, o, sum1.at[h, u, o], in2.at[h, u, o], first[h][o])
+                    ship2[u, o, h].start()
+
+            def sum_first(u):
+                for h in HALVES:
+                    for o in (1, 2, 3):
+                        ship2[u, o, h].wait_recv()
+                    sum2[h, u] = (
+                        (sum1[h, u, 0].astype(F32) + in2[h, u, 1].astype(F32))
+                        + (in2[h, u, 2].astype(F32) + in2[h, u, 3].astype(F32))
+                    ).astype(BF16)
+                    for o in ORDER:
+                        rows_there = pl.ds(pl.multiple_of(turn(other[h], o) * quarter, quarter), quarter)
+                        ship3[u, o, h] = copy(2, h, u, o, sum2.at[h, u, rows_there], in3.at[h, u, o], second[h][o])
+                        ship3[u, o, h].start()
+
+            def sum_second(u):
+                for h in HALVES:
+                    for o in (1, 2, 3):
+                        ship3[u, o, h].wait_recv()
+                    mine_rows = pl.ds(pl.multiple_of(other[h] * quarter, quarter), quarter)
+                    here = pl.ds(pl.multiple_of(h * half + other[h] * quarter, quarter), quarter)
+                    total = (sum2[h, u, mine_rows].astype(F32) + in3[h, u, 1].astype(F32)) + (
+                        in3[h, u, 2].astype(F32) + in3[h, u, 3].astype(F32)
+                    )
+                    at = index_of(c, place[h], u)
+                    full[at, here, :] = total.astype(BF16)
+                    for o in ORDER:
+                        spot = full.at[at, here]
+                        ship4[u, o, h] = copy(3, h, u, o, spot, spot, second[h][o])
+                        ship4[u, o, h].start()
+
+            def origin(o, h):
+                return turn(place[h], (4 - o) % 4)
+
+            def hand_over(u, o, h):
+                spot = full.at[index_of(c, origin(o, h), u), pl.ds(h * half, half)]
+                ship6[u, o, h] = copy(5, h, u, o, spot, spot, sibling)
+                ship6[u, o, h].start()
+
+            def spread(u):
+                for h in HALVES:
+                    for o in (1, 2, 3):
+                        ship4[u, o, h].wait_recv()
+                    spot = full.at[index_of(c, place[h], u), pl.ds(h * half, half)]
+                    hand_over(u, 0, h)
+                    for o in ORDER:
+                        ship5[u, o, h] = copy(4, h, u, o, spot, spot, first[h][o])
+                        ship5[u, o, h].start()
+
+            def collect(u, o):
+                for h in HALVES:
+                    ship5[u, o, h].wait_recv()
+                    hand_over(u, o, h)
+
+            def absorb(u, o, start=False):
+                for h in HALVES:
+                    ship6[u, o, h].wait_recv()
+                    cols = slice(h * half, (h + 1) * half)
+                    q = origin(o, h)
+                    blocks = [full[index_of(core, q, u), h * half : (h + 1) * half, :] for core in (c, sib)]
+                    square = mm(blocks[0], blocks[0], NT) + mm(blocks[1], blocks[1], NT)
+                    if start:
+                        gram_ref[h] = square
+                    else:
+                        gram_ref[h] += square
+                    for r in range(0, rows, part_rows):
+                        at = slice(r, r + part_rows)
+                        term = mm(w_ref[at, columns_of(c, q, u)], blocks[0], NT) + mm(
+                            w_ref[at, columns_of(sib, q, u)], blocks[1], NT
+                        )
+                        if start:
+                            proj[at, cols] = term
+                        else:
+                            proj[at, cols] += term
 
             for i in range(len(steps) + LAG):
                 if i < len(steps):
                     give(*steps[i])
                 if i >= LAG:
                     take(*steps[i - LAG])
-            for h in HALVES:
-                for o in (1, 2, 3):
-                    ship2[o, h].wait_recv()
-                sum2[h] = (
-                    (sum1[h, 0].astype(F32) + in2[h, 1].astype(F32))
-                    + (in2[h, 2].astype(F32) + in2[h, 3].astype(F32))
-                ).astype(BF16)
-                for o in ORDER:
-                    rows_there = pl.ds(pl.multiple_of(turn(other[h], o) * quarter, quarter), quarter)
-                    ship3[o, h] = copy(2, h, o, sum2.at[h, rows_there], in3.at[h, o], second[h][o])
-                    ship3[o, h].start()
-            for h in HALVES:
-                for o in (1, 2, 3):
-                    ship3[o, h].wait_recv()
-                mine_rows = pl.ds(pl.multiple_of(other[h] * quarter, quarter), quarter)
-                here = pl.ds(pl.multiple_of(h * half + other[h] * quarter, quarter), quarter)
-                total = (sum2[h, mine_rows].astype(F32) + in3[h, 1].astype(F32)) + (
-                    in3[h, 2].astype(F32) + in3[h, 3].astype(F32)
-                )
-                spot = full.at[c * 4 + place[h], here]
-                full[c * 4 + place[h], here, :] = total.astype(BF16)
-                for o in ORDER:
-                    ship4[o, h] = copy(3, h, o, spot, spot, second[h][o])
-                    ship4[o, h].start()
-
-            def spot_of(core, q, h):
-                return full.at[core * 4 + q, pl.ds(h * half, half)]
-
-            def absorb(core, q, h, start):
-                cols = slice(h * half, (h + 1) * half)
-                block = full[core * 4 + q, h * half : (h + 1) * half, :]
-                square = mm(block, block, NT)
-                if start:
-                    gram_ref[h] = square
-                else:
-                    gram_ref[h] += square
-                for r in range(parts):
-                    at = slice(r * part_rows, (r + 1) * part_rows)
-                    term = mm(w_ref[r, :, columns_of(core * 4 + q)], block, NT)
-                    if start:
-                        proj[at, cols] = term
-                    else:
-                        proj[at, cols] += term
-
-            for h in HALVES:
-                for o in (1, 2, 3):
-                    ship4[o, h].wait_recv()
-                spot = spot_of(c, place[h], h)
-                for o in ORDER:
-                    ship5[o, h] = copy(4, h, o, spot, spot, first[h][o])
-                    ship5[o, h].start()
-                ship6[0, h] = copy(5, h, 0, spot, spot, sibling)
-                ship6[0, h].start()
-            for h in HALVES:
-                absorb(c, place[h], h, True)
-            for h in HALVES:
-                ship6[0, h].wait_recv()
-                absorb(sib, place[h], h, False)
-            for o in AORDER:
-                for h in HALVES:
-                    q = turn(place[h], 4 - o)
-                    ship5[o, h].wait_recv()
-                    spot = spot_of(c, q, h)
-                    ship6[o, h] = copy(5, h, o, spot, spot, sibling)
-                    ship6[o, h].start()
-                for h in HALVES:
-                    absorb(c, turn(place[h], 4 - o), h, False)
-                for h in HALVES:
-                    ship6[o, h].wait_recv()
-                    absorb(sib, turn(place[h], 4 - o), h, False)
+            sum_first(0)
+            for u in range(CUTS):
+                sum_second(u)
+                if u + 1 < CUTS:
+                    sum_first(u + 1)
+                spread(u)
+            waiting = []
+            for u in range(CUTS):
+                waiting.append((u, 0))
+            absorb(0, 0, True)
+            waiting = waiting[1:]
+            for u in range(CUTS):
+                for o in AORDER:
+                    collect(u, o)
+                    waiting.append((u, o))
+                    absorb(*waiting.pop(0))
+            for item in waiting:
+                absorb(*item)
 
             cross_gram = None
-            for d in range(8):
+            for d in range(8 * CUTS):
                 term = mm(full[d, 0:half, :], full[d, half:rank, :], NT)
                 cross_gram = term if cross_gram is None else cross_gram + term
             gram = jnp.concatenate(
@@ -316,16 +337,14 @@
 
             @pl.when(it + 1 < ITERS)
             def _():
-                for r in range(parts):
-                    at = slice(r * part_rows, (r + 1) * part_rows)
-                    proj_t[:, at] = (mm3(root, split(proj[at, :]), NT) * scale).astype(BF16)
-
-            for o, h in steps:
-                ship1[o, h].wait_send()
-                ship6[o, h].wait_send()
-                if o:
+                proj_t[...] = (mm3(root, split(proj[...]), NT) * scale).astype(BF16)
+
+            for step in steps:
+                ship1[step].wait_send()
+                ship6[step].wait_send()
+                if step[1]:
                     for ship in (ship2, ship3, ship4, ship5):
-                        ship[o, h].wait_send()
+                        ship[step].wait_send()
             return carry
 
         lax.fori_loop(0, ITERS, sweep, 0)
@@ -335,7 +354,8 @@
         for r in range(parts):
             value = mm3(split(proj[r * part_rows : (r + 1) * part_rows, :]), root) * scale
             coef_ref[:, r * ROW : (r + 1) * ROW, :] = value.astype(BF16).reshape(capacity, ROW, rank)
-        block = full[m // 4, :, pl.ds(pl.multiple_of(lax.rem(m, 4) * 128, 128), 128)]
+        per = chunk // 128
+        block = full[m // per, :, pl.ds(pl.multiple_of(lax.rem(m, per) * 128, 128), 128)]
         turned = mm(eye(128).astype(BF16), block, NT).astype(BF16)
         basis_ref[...] = ((mm(turned, root[0]) + mm(turned, root[1])) * scale).astype(BF16)
         for ci in range(total):
@@ -351,17 +371,17 @@
         in_specs=[pl.BlockSpec(memory_space=pltpu.SMEM)] + [pl.BlockSpec(memory_space=pl.ANY)] * 2,
         out_specs=(pl.BlockSpec(memory_space=pltpu.VMEM),) * 2,
         scratch_shapes=[
-            pltpu.VMEM((parts, part_rows, depth), BF16),
+            pltpu.VMEM((rows, depth), BF16),
             pltpu.VMEM((depth, rank), BF16),
             pltpu.VMEM((rows, rank), F32),
             pltpu.VMEM((rank, rows), BF16),
-            pltpu.VMEM((8, rank, chunk), BF16),
-            pltpu.VMEM((2, 4, half, chunk), BF16),
-            pltpu.VMEM((2, 4, half, chunk), BF16),
-            pltpu.VMEM((2, 4, half, chunk), BF16),
-            pltpu.VMEM((2, 4, half, chunk), BF16),
-            pltpu.VMEM((2, half, chunk), BF16),
-            pltpu.VMEM((2, 4, quarter, chunk), BF16),
+            pltpu.VMEM((8 * CUTS, rank, chunk), BF16),
+            pltpu.VMEM((2, CUTS, 4, half, chunk), BF16),
+            pltpu.VMEM((2, CUTS, 4, half, chunk), BF16),
+            pltpu.VMEM((2, CUTS, 4, half, chunk), BF16),
+            pltpu.VMEM((2, CUTS, 4, half, chunk), BF16),
+            pltpu.VMEM((2, CUTS, half, chunk), BF16),
+            pltpu.VMEM((2, CUTS, 4, quarter, chunk), BF16),
             pltpu.VMEM((rank, rank), BF16),
             pltpu.VMEM((rank, rank), BF16),
             pltpu.VMEM((2, half, half), F32),
@@ -373,8 +393,8 @@
             pltpu.SemaphoreType.DMA((total,)),
             pltpu.SemaphoreType.DMA((total, groups)),
             pltpu.SemaphoreType.DMA((total, groups)),
-            pltpu.SemaphoreType.DMA((6, 2, 4)),
-            pltpu.SemaphoreType.DMA((6, 2, 4)),
+            pltpu.SemaphoreType.DMA((6, 2, CUTS, 4)),
+            pltpu.SemaphoreType.DMA((6, 2, CUTS, 4)),
         ]
         + [pltpu.VMEM((experts + 1, ROW, width), BF16) for _, _, width in CHUNKS]
         + [pltpu.VMEM((groups, part_rows, width), BF16) for _, _, width in CHUNKS],

time: 258 us -> 254 us (0.984)
  Pallas kernels: 250 us -> 246 us
    pallas_call x1, Pallas kernels: 250 us -> 246 us  [fit(): pl.pallas_call(kernel, out_shape=(jax.ShapeDtypeStruct((128, rank), BF16)...]
where the time goes in v3:
time: 254 us
  Pallas kernels  246 us (97%)
  local copies, waits for them, and re-layouts  3.93 us (2%)
  other arithmetic  3.03 us (1%)
    pallas_call x1, Pallas kernels, fit(): pl.pallas_call(kernel, out_shape=(jax.ShapeDtypeStruct((128, rank), BF16)...  246 us

profile of v3, /device:TPU:1, one launch (start us, length us, event | category | flops | bytes accessed | tf_op | source)
XLA Modules:
  0.0 254.0 jit_solution(4461328834070435505)
XLA Ops:
  0.6 0.9 convert_reduce_fusion
  1.5 0.7 multiply_add_fusion
  2.2 0.8 select_reduce_fusion.1
  3.1 0.1 select_reduce_fusion
  3.2 0.5 broadcast_add_fusion.sources_ref
  3.7 246.4 %fit.1 = (bf16[128,512]{1,0:T(8,128)(2,1)}, bf16[24,48,512]{2,1,0:T(8,128)(2,1)}) custom-call(s32[96]{0:T(128)} %broadcast_add_fusion.sources_ref, bf16[2,1536,1024]{2,1,0:T(8,128)(2,1)} %weights_ref.1, bf16[4096,512]{1,0:T(8,128)(2,1)} %bitcast.7), custom_call_target="tpu_custom_call" | custom-call | flops 64424509440 | bytes 16777216 | tf_op jit(solution)/shard_map/fit/pallas_call | solution.py:365
  250.1 1.6 copy.8
  251.7 2.4 copy.9
  (1 shorter events, 0.0 us)

commit v4 on v3

--- a/solution.py
+++ b/solution.py
@@ -31,13 +31,12 @@
     assign = assignment[:, 0]
     experts = assign.shape[0]
     ids = jnp.arange(experts, dtype=jnp.int32)
-    same = (assign[None, :] == assign[:, None]) & (ids[None, :] < ids[:, None])
-    slot = assign * capacity + jnp.sum(same.astype(jnp.int32), axis=1)
-    held = (stored_order[:, None] == ids[None, :]).astype(jnp.int32)
-    slot_of_position = jnp.sum(held * slot[None, :], axis=1)
+    before = (assign[None, :] == assign[:, None]) & (ids[None, :] < ids[:, None])
+    whole = jnp.where(ids[None, :] < assign[:, None], capacity, 0)
+    slot = jnp.sum(whole + before.astype(jnp.int32), axis=1)
+    slot_of_position = jnp.sum(jnp.where(stored_order[:, None] == ids[None, :], slot[None, :], 0), axis=1)
     slots = jnp.arange(groups * capacity, dtype=jnp.int32)
-    hit = (slot_of_position[None, :] == slots[:, None]).astype(jnp.int32)
-    return experts + jnp.sum(hit * (ids - experts)[None, :], axis=1)
+    return jnp.min(jnp.where(slot_of_position[None, :] == slots[:, None], ids[None, :], experts), axis=1)
 
 
 NN = (((1,), (0,)), ((), ()))

time: 254 us -> 254 us (level)
  no operation moved by 1% of the time
where the time goes in v4:
time: 254 us; the launch traced here: 253 us
  Pallas kernels  246 us (97%)
  local copies, waits for them, and re-layouts  3.93 us (2%)
    pallas_call x1, Pallas kernels, fit(): pl.pallas_call(kernel, out_shape=(jax.ShapeDtypeStruct((128, rank), BF16)...  246 us

profile of v4, /device:TPU:1, one launch (start us, length us, event | category | flops | bytes accessed | tf_op | source)
XLA Modules:
  0.0 253.3 jit_solution(5890634109913720173)
XLA Ops:
  0.6 0.9 add_reduce_fusion
  1.5 0.8 select_reduce_fusion.1
  2.4 0.6 select_reduce_fusion.sources_ref
  3.0 246.4 %fit.1 = (bf16[128,512]{1,0:T(8,128)(2,1)}, bf16[24,48,512]{2,1,0:T(8,128)(2,1)}) custom-call(s32[96]{0:T(128)} %select_reduce_fusion.sources_ref, bf16[2,1536,1024]{2,1,0:T(8,128)(2,1)} %weights_ref.1, bf16[4096,512]{1,0:T(8,128)(2,1)} %bitcast.6), custom_call_target="tpu_custom_call" | custom-call | flops 64424509440 | bytes 16777216 | tf_op jit(solution)/shard_map/fit/pallas_call | solution.py:364
  249.4 1.6 copy.8
  251.0 2.4 copy.9

commit v5 on v4

--- a/solution.py
+++ b/solution.py
@@ -303,6 +303,11 @@
                 if u + 1 < CUTS:
                     sum_first(u + 1)
                 spread(u)
+            for step in steps:
+                ship1[step].wait_send()
+                if step[1]:
+                    for ship in (ship2, ship3):
+                        ship[step].wait_send()
             waiting = []
             for u in range(CUTS):
                 waiting.append((u, 0))
@@ -339,10 +344,9 @@
                 proj_t[...] = (mm3(root, split(proj[...]), NT) * scale).astype(BF16)
 
             for step in steps:
-                ship1[step].wait_send()
                 ship6[step].wait_send()
                 if step[1]:
-                    for ship in (ship2, ship3, ship4, ship5):
+                    for ship in (ship4, ship5):
                         ship[step].wait_send()
             return carry
 

time: 254 us -> 254 us (level)
  no operation moved by 1% of the time
where the time goes in v5:
time: 254 us; the launch traced here: 253 us
  Pallas kernels  246 us (97%)
  local copies, waits for them, and re-layouts  3.93 us (2%)
    pallas_call x1, Pallas kernels, fit(): pl.pallas_call(kernel, out_shape=(jax.ShapeDtypeStruct((128, rank), BF16)...  246 us

profile of v5, /device:TPU:1, one launch (start us, length us, event | category | flops | bytes accessed | tf_op | source)
XLA Modules:
  0.0 253.3 jit_solution(8831369821219536594)
XLA Ops:
  0.6 0.9 add_reduce_fusion
  1.5 0.8 select_reduce_fusion.1
  2.4 0.6 select_reduce_fusion.sources_ref
  3.0 246.3 %fit.1 = (bf16[128,512]{1,0:T(8,128)(2,1)}, bf16[24,48,512]{2,1,0:T(8,128)(2,1)}) custom-call(s32[96]{0:T(128)} %select_reduce_fusion.sources_ref, bf16[2,1536,1024]{2,1,0:T(8,128)(2,1)} %weights_ref.1, bf16[4096,512]{1,0:T(8,128)(2,1)} %bitcast.6), custom_call_target="tpu_custom_call" | custom-call | flops 64424509440 | bytes 16777216 | tf_op jit(solution)/shard_map/fit/pallas_call | solution.py:368
  249.3 1.6 copy.8
  250.9 2.4 copy.9
